TPU v7x, 32 devices: a whole 2x2x4 slice. The times are simulated.
32 devices in a mesh: blk: 8 (over z, y), dp: 4 (over x, core).
Axes of the slice: x: 2, y: 2, z: 4, core: 2. Of those that a mesh axis runs over, the one named last changes fastest.
Arguments:
- tokens: bfloat16 [4, 3072, 640], P('dp', 'blk'), may hold values from -6 to 6
- lengths: int32 [4, 4], P('dp'), may hold values from 0 to 3072, as said below
- cotangent: bfloat16 [4, 3072, 640], P('dp', 'blk'), may hold values from -6 to 6
- norm_in: float32 [640], replicated, may hold values from 0.1 to 1.9
- w_query: bfloat16 [640, 1024], replicated, may hold values from -0.25 to 0.25
- w_key: bfloat16 [640, 256], replicated, may hold values from -0.25 to 0.25
- w_value: bfloat16 [640, 256], replicated, may hold values from -0.25 to 0.25
- query_gain: float32 [256], replicated, may hold values from 0.1 to 1.9
- key_gain: float32 [256], replicated, may hold values from 0.1 to 1.9
- w_out: bfloat16 [1024, 640], replicated, may hold values from -0.1875 to 0.1875
- norm_attn: float32 [640], replicated, may hold values from 0.1 to 1.9
- norm_pre: float32 [640], replicated, may hold values from 0.1 to 1.9
- w_gate: bfloat16 [640, 2048], replicated, may hold values from -0.25 to 0.25
- w_up: bfloat16 [640, 2048], replicated, may hold values from -0.25 to 0.25
- w_down: bfloat16 [2048, 640], replicated, may hold values from -0.125 to 0.125
- norm_post: float32 [640], replicated, may hold values from 0.1 to 1.9
Outputs:
- output: bfloat16 [4, 3072, 640], P('dp', 'blk')
- input_grad: bfloat16 [4, 3072, 640], P('dp', 'blk')
- grad_norm_in: float32 [640], replicated
- grad_query: float32 [640, 1024], replicated
- grad_key: float32 [640, 256], replicated
- grad_value: float32 [640, 256], replicated
- grad_query_gain: float32 [256], replicated
- grad_key_gain: float32 [256], replicated
- grad_out: float32 [1024, 640], replicated
- grad_norm_attn: float32 [640], replicated
- grad_norm_pre: float32 [640], replicated
- grad_gate: float32 [640, 2048], replicated
- grad_up: float32 [640, 2048], replicated
- grad_down: float32 [2048, 640], replicated
- grad_norm_post: float32 [640], replicated
Inputs may be any that keep to these rules, and one draw needn't show every extreme that they name: Each row holds the lengths of a group's sequences in order, summing to 3072: one, two or four positive lengths followed by zeros; some group in every draw is a single sequence of 3072 tokens.
All inputs are finite; a program needn't handle non-finite values.
Results may differ from a plain program's by a relative error of at most 0.025.
Values may be sent and summed in bfloat16 or wider, within the bound.
A program may use at most 192 MiB of HBM per device.

v0:
```python
import functools

import jax
import jax.numpy as jnp
from jax import lax
from jax.experimental import pallas as pl
from jax.experimental.pallas import tpu as pltpu
from jax.sharding import PartitionSpec as P

BLOCKS, PARTS = "blk", "dp"
EPS = 1e-06
BASE = 1000000.0
NEG = -1e30


def shifted(array, axis, by):
    peers = lax.axis_size(axis)
    return lax.ppermute(array, axis, [(i, (i + by) % peers) for i in range(peers)])


def from_behind(block, axis, distance):
    devices = range(lax.axis_size(axis))
    route = [(i - distance, i) for i in devices if i - distance in devices]
    return lax.ppermute(block, axis, route)


def normed(value, gain):
    return value * lax.rsqrt(jnp.mean(value * value, axis=-1, keepdims=True) + EPS) * gain


def normed_back(value, gain, grad):
    return jax.vjp(normed, value, gain)[1](grad)


def segment_of(index, row):
    ends = jnp.cumsum(row)
    seg = jnp.sum((index[:, None] >= ends[None, :]).astype(jnp.int32), axis=1)
    starts = ends - row
    slots = jnp.arange(row.shape[0], dtype=jnp.int32)
    begin = jnp.sum(jnp.where(slots[None, :] == seg[:, None], starts[None, :], 0), axis=1)
    return (seg, index - begin)


def rotary_tables(places, head):
    half = head // 2
    freq = jnp.exp(-(2.0 * jnp.arange(half, dtype=jnp.float32) / head) * jnp.log(BASE))
    angle = places.astype(jnp.float32)[:, None] * freq[None, :]
    return (jnp.cos(angle), jnp.sin(angle))


def prepare(proj, gain, cosine, sine):
    value = normed(proj, gain)
    half = value.shape[-1] // 2
    first = value[..., :half]
    second = value[..., half:]
    return jnp.concatenate(
        [first * cosine - second * sine, second * cosine + first * sine], axis=-1
    )


def pass_home(grads):
    return shifted(grads.astype(jnp.bfloat16), BLOCKS, 1).astype(grads.dtype)


MESH = pl.DeviceIdType.MESH


def where_am_i():
    place = lax.axis_index(BLOCKS)
    part = lax.axis_index(PARTS)
    return {
        "z": place // 2,
        "y": lax.rem(place, 2),
        "x": part // 2,
        "core": lax.rem(part, 2),
        "place": place,
        "part": part,
    }


def peers_of(me):
    place, part = me["place"], me["part"]
    return {
        "core": {BLOCKS: place, PARTS: part + 1 - 2 * me["core"]},
        "x": {BLOCKS: place, PARTS: part + 2 - 4 * me["x"]},
        "y": {BLOCKS: place + 1 - 2 * me["y"], PARTS: part},
        "up": {BLOCKS: place + 2, PARTS: part},
        "down": {BLOCKS: place - 2, PARTS: part},
    }


def greet(me, peers, z_count):
    barrier = pltpu.get_barrier_semaphore()
    for name in ("core", "x", "y"):
        pl.semaphore_signal(barrier, inc=1, device_id=peers[name], device_id_type=MESH)

    @pl.when(me["z"] < z_count - 1)
    def _():
        pl.semaphore_signal(barrier, inc=1, device_id=peers["up"], device_id_type=MESH)

    @pl.when(me["z"] > 0)
    def _():
        pl.semaphore_signal(barrier, inc=1, device_id=peers["down"], device_id_type=MESH)

    ends = (me["z"] == 0).astype(jnp.int32) + (me["z"] == z_count - 1).astype(jnp.int32)
    pl.semaphore_wait(barrier, 5 - ends)


def add_into(target, start, row, extra, count, rows):
    step = rows if rows < 32 else 16
    for candidate in (160, 128, 80, 64, 48, 32):
        if rows % candidate == 0:
            step = candidate
            break

    def body(index, carry):
        e = index // (rows // step)
        at = pl.multiple_of(lax.rem(index, rows // step) * step, 8)
        here = pl.ds(pl.multiple_of(row + at, 8), step)
        target[start + e, here, :] = target[start + e, here, :] + extra[e, pl.ds(at, step), :]
        return carry

    lax.fori_loop(0, count * (rows // step), body, 0)


STAGES = 10


class Chunk:
    def __init__(self, number, grad, total, row, rows, first, landing, sems, me, peers, z_count):
        self.grad, self.total, self.row, self.rows = grad, total, row, rows
        self.first, self.second = ("x", "y") if first == "x" else ("y", "x")
        self.land0, self.land1, self.land2 = landing
        self.send, self.recv, self.local = sems
        self.number, self.me, self.peers, self.z_count = number, me, peers, z_count
        self.b1, self.b2, self.core = me[self.first], me[self.second], me["core"]
        self.quad = 4 * self.core
        self.pair = self.quad + 2 * self.b1
        self.own = self.pair + self.b2
        self.half = rows // 2

    @staticmethod
    def landing(rows):
        return ((4, rows), (2, rows), (1, 2 * rows))

    def piece(self, start, count, upper=None):
        if upper is None:
            return self.grad.at[pl.ds(start, count), pl.ds(self.row, self.rows), :]
        row = self.row if upper else self.row + self.half
        return self.grad.at[pl.ds(start, count), pl.ds(row, self.half), :]

    def spot(self, count, upper=None):
        row, rows = self.row, self.rows
        if upper is not None:
            row, rows = (row if upper else row + self.half), self.half
        here, columns = pl.ds(row, rows), self.grad.shape[2]
        start = {1: self.own, 2: self.pair, 4: self.quad}[count]
        if len(self.total.shape) == 2:
            return self.total.at[here, pl.ds(pl.multiple_of(start * columns, 128), count * columns)]
        if len(self.total.shape) == 4:
            if count == 4:
                return self.total.at[self.core, :, here, :]
            if count == 2:
                return self.total.at[self.core, self.b1, here, :]
            return self.total.at[self.core, self.b1, here, pl.ds(pl.multiple_of(self.b2 * columns, 128), columns)]
        if count == 1:
            return self.total.at[start, here, :]
        return self.total.at[pl.ds(start, count), here, :]

    def mine(self, upper):
        return self.grad.at[self.own, pl.ds(self.row if upper else self.row + self.half, self.half), :]

    def keep(self, upper):
        return pltpu.make_async_copy(
            self.mine(upper), self.spot(1, upper), self.local.at[self.number]
        )

    def copy(self, stage, peer, source, target):
        return pltpu.make_async_remote_copy(
            src_ref=source,
            dst_ref=target,
            send_sem=self.send.at[self.number, stage],
            recv_sem=self.recv.at[self.number, stage],
            device_id=self.peers[peer],
            device_id_type=MESH,
        )

    def reduce_up(self):
        return self.copy(3, "up", self.piece(self.own, 1, True), self.land2.at[:, pl.ds(self.rows, self.half), :])

    def reduce_down(self):
        return self.copy(4, "down", self.piece(self.own, 1, False), self.land2.at[:, pl.ds(self.rows + self.half, self.half), :])

    def spread_down(self, fresh=False):
        here = self.spot(1, True)
        return self.copy(5, "down", self.mine(True) if fresh else here, here)

    def spread_up(self, fresh=False):
        here = self.spot(1, False)
        return self.copy(6, "up", self.mine(False) if fresh else here, here)

    def step0(self):
        return self.copy(0, "core", self.piece(4 - self.quad, 4), self.land0)

    def step1(self):
        return self.copy(1, self.first, self.piece(self.quad + 2 - 2 * self.b1, 2), self.land1)

    def step2(self):
        return self.copy(2, self.second, self.piece(self.pair + 1 - self.b2, 1), self.land2.at[:, pl.ds(0, self.rows), :])

    def gather(self, stage):
        count, peer = ((1, self.second), (2, self.first), (4, "core"))[stage - 7]
        here = self.spot(count)
        return self.copy(stage, peer, here, here)

    def arrive_upper(self):
        z, last = self.me["z"], self.z_count - 1

        @pl.when(z > 0)
        def _():
            self.reduce_up().wait_recv()
            add_into(self.grad, self.own, self.row, self.land2.at[:, pl.ds(self.rows, self.half), :], 1, self.half)

            @pl.when(z < last)
            def _():
                self.reduce_up().start()

            @pl.when(z == last)
            def _():
                self.spread_down(True).start()
                self.keep(True).start()

    def arrive_lower(self):
        z, last = self.me["z"], self.z_count - 1

        @pl.when(z < last)
        def _():
            self.reduce_down().wait_recv()
            add_into(self.grad, self.own, self.row + self.half, self.land2.at[:, pl.ds(self.rows + self.half, self.half), :], 1, self.half)

            @pl.when(z > 0)
            def _():
                self.reduce_down().start()

            @pl.when(z == 0)
            def _():
                self.spread_up(True).start()
                self.keep(False).start()

    def back_upper(self):
        z, last = self.me["z"], self.z_count - 1

        @pl.when(z < last)
        def _():
            self.spread_down().wait_recv()

            @pl.when(z > 0)
            def _():
                self.spread_down().start()

    def back_lower(self):
        z, last = self.me["z"], self.z_count - 1

        @pl.when(z > 0)
        def _():
            self.spread_up().wait_recv()

            @pl.when(z < last)
            def _():
                self.spread_up().start()

    def tick(self, op):
        z, last = self.me["z"], self.z_count - 1
        if op == 0:
            self.step0().start()
        elif op == 1:
            self.step0().wait_recv()
            add_into(self.grad, self.quad, self.row, self.land0, 4, self.rows)
            self.step1().start()
        elif op == 2:
            self.step1().wait_recv()
            add_into(self.grad, self.pair, self.row, self.land1, 2, self.rows)
            self.step2().start()
        elif op == 3:
            self.step2().wait_recv()
            add_into(self.grad, self.own, self.row, self.land2, 1, self.rows)

            @pl.when(z == 0)
            def _():
                self.reduce_up().start()

            @pl.when(z == last)
            def _():
                self.reduce_down().start()

        elif op == 4:
            pl.when((z > 0) & (2 * z < self.z_count))(self.arrive_upper)
            pl.when((z < last) & (2 * z >= self.z_count))(self.arrive_lower)
        elif op == 5:
            pl.when((z < last) & (2 * z >= self.z_count))(self.arrive_upper)
            pl.when((z > 0) & (2 * z < self.z_count))(self.arrive_lower)
        elif op == 6:
            pl.when(z == last)(self.arrive_upper)
            pl.when(z == 0)(self.arrive_lower)
        elif op == 7:
            pl.when((z < last) & (2 * z >= self.z_count))(self.back_upper)
            pl.when((z > 0) & (2 * z < self.z_count))(self.back_lower)
        elif op == 8:

            @pl.when((z > 0) & (2 * z < self.z_count))
            def _():
                self.back_upper()
                self.gather(7).start()

            @pl.when((z < last) & (2 * z >= self.z_count))
            def _():
                self.back_lower()
                self.gather(7).start()

        elif op == 9:

            @pl.when(z == 0)
            def _():
                self.back_upper()
                self.keep(False).wait()
                self.gather(7).start()

            @pl.when(z == last)
            def _():
                self.back_lower()
                self.keep(True).wait()
                self.gather(7).start()

        elif op == 10:
            self.gather(7).wait_recv()
            self.gather(8).start()
        elif op == 11:
            self.gather(8).wait_recv()
            self.gather(9).start()
        elif op == 12:
            self.gather(9).wait_recv()
            self.drain()

    OPS = 13

    def drain(self):
        z, last = self.me["z"], self.z_count - 1
        self.step0().wait_send()
        self.step1().wait_send()
        self.step2().wait_send()
        for stage in (7, 8, 9):
            self.gather(stage).wait_send()

        @pl.when(z < last)
        def _():
            self.reduce_up().wait_send()
            self.spread_up().wait_send()

        @pl.when(z > 0)
        def _():
            self.reduce_down().wait_send()
            self.spread_down().wait_send()


class LineChunk(Chunk):
    def __init__(self, *args):
        super().__init__(*args[:6], (args[6][0], None, None), *args[7:])
        self.ups, self.downs, self.small = args[6][1:]
        self.entry = self.quad + self.me["z"]
        self.half, self.quarter = self.rows // 2, self.rows // 4
        self.mine_half = pl.multiple_of(self.row + self.b1 * self.half, 16)
        self.mine_quarter = pl.multiple_of(self.mine_half + self.b2 * self.quarter, 16)

    @staticmethod
    def landing(rows):
        return ((4, rows), (3, rows), (3, rows), (1, rows))

    def across(self, stage, name, first, count):
        landing = self.ups if name == "up" else self.downs
        return self.copy(stage, name, self.piece(self.quad + first, count), landing.at[pl.ds(0, count)])

    def back(self, stage, name, first, count):
        here = self.place(self.quad + first, count, self.row, self.rows)
        return self.copy(stage, name, here, here)

    def place(self, start, count, row, rows):
        here, columns = pl.ds(row, rows), self.grad.shape[2]
        if len(self.total.shape) == 2:
            return self.total.at[here, pl.ds(pl.multiple_of(start * columns, 128), count * columns)]
        if count == 1:
            return self.total.at[start, here, :]
        return self.total.at[pl.ds(start, count), here, :]

    def part(self, row, rows):
        return self.grad.at[pl.ds(self.entry, 1), pl.ds(row, rows), :]

    def step1(self):
        other = pl.multiple_of(self.row + (1 - self.b1) * self.half, 16)
        return self.copy(1, self.first, self.part(other, self.half), self.small.at[:, pl.ds(0, self.half), :])

    def step2(self):
        other = pl.multiple_of(self.mine_half + (1 - self.b2) * self.quarter, 16)
        landing = self.small.at[:, pl.ds(self.half, self.quarter), :]
        return self.copy(2, self.second, self.part(other, self.quarter), landing)

    def finished(self):
        return self.grad.at[self.entry, pl.ds(self.mine_quarter, self.quarter), :]

    def keep(self):
        spot = self.place(self.entry, 1, self.mine_quarter, self.quarter)
        return pltpu.make_async_copy(self.finished(), spot, self.local.at[self.number])

    def gather2(self):
        spot = self.place(self.entry, 1, self.mine_quarter, self.quarter)
        return self.copy(7, self.second, self.finished(), spot)

    def gather1(self):
        here = self.place(self.entry, 1, self.mine_half, self.half)
        return self.copy(8, self.first, here, here)

    def gather0(self):
        here = self.place(self.quad, 4, self.row, self.rows)
        return self.copy(9, "core", here, here)

    def at_row(self, k, body):
        pl.when(self.me["z"] == k)(body)

    def from_below(self, k):
        return (k, self.z_count - k)

    def from_above(self, k):
        return (0, k + 1)

    def take_up(self, k):
        first, count = self.from_below(k)
        self.across(3, "up", first, count).wait_recv()
        add_into(self.grad, self.quad + first, self.row, self.ups, count, self.rows)
        if k < self.z_count - 1:
            self.across(3, "up", first + 1, count - 1).start()

    def take_down(self, k):
        first, count = self.from_above(k)
        self.across(4, "down", first, count).wait_recv()
        add_into(self.grad, self.quad + first, self.row, self.downs, count, self.rows)
        if k > 0:
            self.across(4, "down", first, count - 1).start()

    def back_up(self, k):
        self.back(6, "up", 0, k).wait_recv()
        if k < self.z_count - 1:
            self.back(6, "up", 0, k + 1).start()

    def back_down(self, k):
        last = self.z_count - 1
        self.back(5, "down", k + 1, last - k).wait_recv()
        if k > 0:
            self.back(5, "down", k, last - k + 1).start()

    def tick(self, op):
        last, middle = self.z_count - 1, self.z_count // 2
        if op == 0:
            self.step0().start()
        elif op == 1:
            self.step0().wait_recv()
            add_into(self.grad, self.quad, self.row, self.land0, 4, self.rows)
            self.at_row(0, lambda: self.across(3, "up", 1, last).start())
            self.at_row(last, lambda: self.across(4, "down", 0, last).start())
        elif op == 2:
            for k in range(1, last):
                self.at_row(k, functools.partial(self.take_up if k < middle else self.take_down, k))
        elif op == 3:
            for k in range(1, last):

                def arrive(k=k):
                    (self.take_down if k < middle else self.take_up)(k)
                    self.step1().start()

                self.at_row(k, arrive)
        elif op == 4:

            def bottom():
                self.take_down(0)
                self.step1().start()

            def top():
                self.take_up(last)
                self.step1().start()

            self.at_row(0, bottom)
            self.at_row(last, top)
        elif op == 5:
            self.step1().wait_recv()
            add_into(self.grad, self.entry, self.mine_half, self.small, 1, self.half)
            self.step2().start()
        elif op == 6:
            self.step2().wait_recv()
            landing = self.small.at[:, pl.ds(self.half, self.quarter), :]
            add_into(self.grad, self.entry, self.mine_quarter, landing, 1, self.quarter)
            self.keep().start()
            self.gather2().start()
        elif op == 7:
            self.gather2().wait_recv()
            self.keep().wait()
            self.gather1().start()
        elif op == 8:
            self.gather1().wait_recv()
            self.at_row(0, lambda: self.back(6, "up", 0, 1).start())
            self.at_row(last, lambda: self.back(5, "down", last, 1).start())
        elif op == 9:
            for k in range(1, last):
                self.at_row(k, functools.partial(self.back_up if k < middle else self.back_down, k))
        elif op == 10:
            for k in range(1, last):

                def complete(k=k):
                    (self.back_down if k < middle else self.back_up)(k)
                    self.gather0().start()

                self.at_row(k, complete)
        elif op == 11:

            def bottom():
                self.back_down(0)
                self.gather0().start()

            def top():
                self.back_up(last)
                self.gather0().start()

            self.at_row(0, bottom)
            self.at_row(last, top)
        elif op == 12:
            self.gather0().wait_recv()
            self.drain()

    def drain(self):
        last = self.z_count - 1
        for item in (self.step0(), self.step1(), self.step2(), self.gather2(), self.gather1(), self.gather0()):
            item.wait_send()
        for k in range(self.z_count):

            def sent(k=k):
                if k < last:
                    self.across(3, "up", k + 1, last - k).wait_send()
                    self.back(6, "up", 0, k + 1).wait_send()
                if k > 0:
                    self.across(4, "down", 0, k).wait_send()
                    self.back(5, "down", k, last - k + 1).wait_send()

            self.at_row(k, sent)


def sum_kernel(z_count, plan, *refs):
    n = 1 + max(item[0] for item in plan)
    parts = len(plan)
    ins, outs = refs[:n], refs[n : 2 * n]
    rest = refs[2 * n :]
    grads, rest = rest[:n], rest[n:]
    landings = rest[: 3 * parts]
    send, recv, local, load = rest[3 * parts :]
    me = where_am_i()
    peers = peers_of(me)
    loads = [pltpu.make_async_copy(ins[i], grads[i], load.at[i]) for i in range(n)]
    for item in loads:
        item.start()
    greet(me, peers, z_count)
    for item in loads:
        item.wait()
    chunks = []
    for number, (i, row, rows, first) in enumerate(plan):
        landing = landings[3 * number : 3 * number + 3]
        chunks.append(
            Chunk(number, grads[i], outs[i], row, rows, first, landing, (send, recv, local), me, peers, z_count)
        )
    for at in range(parts + Chunk.OPS - 1):
        for number in range(parts):
            if 0 <= at - number < Chunk.OPS:
                chunks[number].tick(at - number)


def sum_call(arrays, plan, z_count):
    landing = []
    for i, row, rows, first in plan:
        columns, kind = arrays[i].shape[2], arrays[i].dtype
        landing += [
            pltpu.VMEM((4, rows, columns), kind),
            pltpu.VMEM((2, rows, columns), kind),
            pltpu.VMEM((1, 2 * rows, columns), kind),
        ]
    n = len(arrays)
    return pl.pallas_call(
        functools.partial(sum_kernel, z_count, plan),
        out_shape=tuple(jax.ShapeDtypeStruct(v.shape, v.dtype) for v in arrays),
        in_specs=[pl.BlockSpec(memory_space=pl.ANY)] * n,
        out_specs=tuple([pl.BlockSpec(memory_space=pl.ANY)] * n),
        scratch_shapes=[pltpu.VMEM(v.shape, v.dtype) for v in arrays]
        + landing
        + [
            pltpu.SemaphoreType.DMA((len(plan), STAGES)),
            pltpu.SemaphoreType.DMA((len(plan), STAGES)),
            pltpu.SemaphoreType.DMA((len(plan),)),
            pltpu.SemaphoreType.DMA((n,)),
        ],
        compiler_params=pltpu.CompilerParams(
            collective_id=0, has_side_effects=True, vmem_limit_bytes=56 * 2**20
        ),
    )(*arrays)


def columns_to_panels(value):
    rows, columns = value.shape
    return jnp.transpose(value.reshape(rows, 8, columns // 8), (1, 0, 2)).astype(jnp.bfloat16)


def panels_to_columns(panels):
    count, rows, width = panels.shape
    return jnp.transpose(panels.astype(jnp.float32), (1, 0, 2)).reshape(rows, count * width)


def sum_gradients(grads):
    (g_in, g_query, g_key, g_value, g_qgain, g_kgain, g_out, g_attn, g_pre, g_gate, g_up, g_down, g_post) = grads
    z_count = lax.axis_size(BLOCKS) // 2
    width = g_in.shape[0]
    gains = [g_in, g_attn, g_pre, g_post, g_qgain, g_kgain]
    sizes = [v.shape[0] for v in gains]
    flat = jnp.concatenate(gains)
    gain_rows = 32
    flat = jnp.pad(flat, (0, 8 * gain_rows * 128 - flat.shape[0])).reshape(8, gain_rows, 128)
    down = g_down.astype(jnp.bfloat16).reshape(8, -1, width)
    out = g_out.astype(jnp.bfloat16).reshape(8, -1, width)
    both = jnp.stack([g_key, g_value])
    head = g_key.shape[1]
    both = jnp.transpose(both.reshape(2, 2, width // 2, 2, head // 2), (0, 1, 3, 2, 4)).reshape(8, width // 2, head // 2)
    arrays = [down, columns_to_panels(g_gate), columns_to_panels(g_up), out, columns_to_panels(g_query), both.astype(jnp.bfloat16), flat]
    plan = []
    for i, v in enumerate(arrays[:-1]):
        rows = v.shape[1] // 2
        plan += [(i, 0, rows, "x"), (i, rows, rows, "y")]
    plan.append((6, 0, gain_rows, "x"))
    down, gate, up, out, query, both, flat = sum_call(arrays, plan, z_count)
    both = jnp.transpose(both.astype(jnp.float32).reshape(2, 2, 2, width // 2, head // 2), (0, 1, 3, 2, 4)).reshape(2, width, head)
    flat = flat.reshape(-1)
    cuts, at = [], 0
    for size in sizes:
        cuts.append(flat[at : at + size])
        at += size
    g_in, g_attn, g_pre, g_post, g_qgain, g_kgain = cuts
    return (
        g_in,
        panels_to_columns(query),
        both[0],
        both[1],
        g_qgain,
        g_kgain,
        out.astype(jnp.float32).reshape(g_out.shape),
        g_attn,
        g_pre,
        panels_to_columns(gate),
        panels_to_columns(up),
        down.astype(jnp.float32).reshape(g_down.shape),
        g_post,
    )


LOG2E = 1.4426950408889634
LN2 = 0.6931471805599453
PIECES = (2, 2, 2, 2, 2, 2, 1)
FIRST = ['y', 'y', 'x', 'v', 'x', 'y', 'x', 'x', 'x', 'y', 'x', 'y', 'y']
SCHEDULES = {
    4: (
        (1, 0), (0, 0), ("S", 0), ("F", 0), (1, 1), ("F", 1), (4, 0), ("M", 0), (4, 1), (3, 0), (0, 1), ("O", 0), (1, 2), (3, 1), ("V", 0), (0, 2),
        (4, 2), (2, 0), (7, 0), (5, 0), ("V", 1), (3, 2), (1, 3), (6, 0), (0, 3), ("V", 2), (2, 1), (5, 1), (0, 4), (1, 4), (4, 3), (4, 4), (7, 1),
        (1, 5), (0, 5), (4, 5), (6, 1), (3, 3), ("P", 0), ("P", 1), ("V", 3), (0, 6), (1, 6), ("P", 2), ("Q", 0), ("Q", 1), (7, 2), (4, 6), (5, 2),
        ("Q", 2), (1, 7), ("Q", 3), (6, 2), (3, 4), ("G", 0), (0, 7), (8, 0), (1, 8), (2, 2), (9, 0), (5, 3), ("T", 0), (8, 1), (4, 7), (7, 3),
        ("K", 0), (4, 8), (1, 9), (0, 8), (5, 4), (10, 0), (6, 3), (7, 4), (9, 1), (12, 0), (3, 5), (8, 2), (6, 4), (5, 5), (7, 5), (2, 3), (10, 1),
        (11, 0), (6, 5), (12, 1), (2, 4), (3, 6), (11, 1), (9, 2), (10, 2), (5, 6), (12, 2), (7, 6), (4, 9), (6, 6), (5, 7), (3, 7), (2, 5), (1, 10),
        (11, 2), (6, 7), (12, 3), (8, 3), (0, 9), (7, 7), (12, 4), (8, 4), (10, 3), (9, 3), (5, 8), (10, 4), (9, 4), (11, 3), (4, 10), (2, 6),
        (11, 4), (7, 8), (3, 8), (6, 8), (8, 5), (5, 9), (12, 5), (10, 5), (7, 9), (6, 9), (11, 5), (8, 6), (9, 5), (0, 10), (12, 6), (2, 7), (11, 6),
        (12, 7), (10, 6), (8, 7), (10, 7), (9, 6), (7, 10), (11, 7), (9, 7), (3, 9), (6, 10), (8, 8), (1, 11), (10, 8), (2, 8), (8, 9), (2, 9),
        (12, 8), (12, 9), (10, 9), (9, 8), (11, 8), (9, 9), (5, 10), (7, 11), (11, 9), (4, 11), (12, 10), (8, 10), (3, 10), (0, 11), (11, 10),
        (7, 12), (10, 10), (2, 10), (4, 12), (9, 10), (6, 11), (8, 11), (10, 11), (5, 11), (12, 11), (11, 11), (8, 12), (3, 11), (2, 11), (12, 12),
        (11, 12), (9, 11), (1, 12), (2, 12), (0, 12), (5, 12), (3, 12), (9, 12), (6, 12), (10, 12),
    )
}


def dot(left, right):
    return jnp.dot(left, right, preferred_element_type=jnp.float32)


def dot_nt(left, right):
    return lax.dot_general(left, right, (((1,), (1,)), ((), ())), preferred_element_type=jnp.float32)


def inverse_rms(value):
    return lax.rsqrt(jnp.mean(value * value, axis=-1, keepdims=True) + EPS)


def rms_back(value, inverse, gain, grad):
    scaled = grad * gain
    normal = value * inverse
    mean = jnp.mean(scaled * normal, axis=-1, keepdims=True)
    terms = grad * normal
    return inverse * (scaled - normal * mean), jnp.sum(terms.reshape(-1, 8, terms.shape[-1]), axis=0)


def turn(value, cosine, sine):
    half = value.shape[-1] // 2
    first, second = value[:, :half], value[:, half:]
    return jnp.concatenate([first * cosine - second * sine, second * cosine + first * sine], axis=-1)


def turn_back(grad, cosine, sine):
    half = grad.shape[-1] // 2
    first, second = grad[:, :half], grad[:, half:]
    return jnp.concatenate([first * cosine + second * sine, second * cosine - first * sine], axis=-1)


def dot_tn(left, right):
    return lax.dot_general(left, right, (((0,), (0,)), ((), ())), preferred_element_type=jnp.float32)


def bf16(value):
    return value.astype(jnp.bfloat16)


def f32(value):
    return value.astype(jnp.float32)


class Names(dict):
    __getattr__ = dict.__getitem__


def layer_kernel(sizes, schedule, names, *refs):
    r = Names(zip(names, refs, strict=True))
    rows, width, hidden, heads, head, z_count = sizes
    scale = head**-0.5
    tile = 128
    tiles = [slice(at, at + tile) for at in range(0, rows, tile)]
    half = head // 2
    me = where_am_i()
    peers = peers_of(me)
    z, y, place = me["z"], me["y"], me["place"]
    last = z_count - 1

    weights = ["x", "w_key", "w_value", "w_query", "w_out", "w_gate", "w_up", "w_down", "dy"]
    joined = heads * head
    wide_k, wide_v = slice(joined, joined + head), slice(joined + head, joined + 2 * head)
    spots = {"w_query": slice(0, joined), "w_key": wide_k, "w_value": wide_v}
    pair = ("w_gate", "w_up")
    loads = {}
    for i, name in enumerate(weights):
        if name in spots:
            spot = r.w_first.at[:, spots[name]]
        elif name in pair:
            spot = r.w_pair.at[pair.index(name)]
        else:
            spot = r[name]
        loads[name] = pltpu.make_async_copy(r[name + "_in"], spot, r.load_sem.at[i])
    early = ("x", "w_key", "w_value")
    for name in early:
        loads[name].start()
    greet(me, peers, z_count)

    def begins(token):
        begin, end = jnp.zeros_like(token), jnp.int32(0)
        for j in range(r.lengths.shape[1]):
            end = end + r.lengths[0, j]
            begin = jnp.where(token >= end, end, begin)
        return begin

    token = place * rows + lax.broadcasted_iota(jnp.int32, (1, rows), 1)
    begin = begins(token)
    entry = f32(lax.broadcasted_iota(jnp.int32, (1, half), 1))
    speed = jnp.exp(-(2.0 * entry / head) * jnp.log(BASE))
    for t in tiles:
        column = place * rows + t.start + lax.broadcasted_iota(jnp.int32, (tile, 1), 0)
        angle = f32(column - begins(column)) * speed
        r.cosine[t, :] = jnp.cos(angle)
        r.sine[t, :] = jnp.sin(angle)
    gain_in = r.norm_in[...].reshape(1, width)
    gain_q = r.query_gain[...].reshape(1, head)
    gain_k = r.key_gain[...].reshape(1, head)
    gain_attn = r.norm_attn[...].reshape(1, width)
    gain_pre = r.norm_pre[...].reshape(1, width)
    gain_post = r.norm_post[...].reshape(1, width)

    def allowed(source):
        key = source * rows + lax.broadcasted_iota(jnp.int32, (rows, rows), 0)
        return (key >= begin) & (key <= token)

    loads["x"].wait()
    loads["w_key"].wait()
    loads["w_value"].wait()
    for name in weights:
        if name not in early:
            loads[name].start()
    for t in tiles:
        x = f32(r.x[t, :])
        r.a[t, :] = bf16(x * inverse_rms(x) * gain_in)
    r.kp[...] = dot(r.a[...], r.w_first[:, wide_k])
    r.kv[place, :, head : 2 * head] = bf16(dot(r.a[...], r.w_first[:, wide_v]))
    for t in tiles:
        kp = r.kp[t, :]
        r.kv[place, t, 0:head] = bf16(turn(kp * inverse_rms(kp) * gain_k, r.cosine[t, :], r.sine[t, :]))

    def send_kv(source, route):
        return pltpu.make_async_remote_copy(
            src_ref=r.kv.at[source],
            dst_ref=r.kv.at[source],
            send_sem=r.kv_send.at[route, source],
            recv_sem=r.kv_recv.at[source],
            device_id=peers["y"] if route else peers["up"],
            device_id_type=MESH,
        )

    def send_half(values):
        half_block = r.kv.at[0, :, head * values : head * (values + 1)]
        return pltpu.make_async_remote_copy(
            src_ref=half_block,
            dst_ref=half_block,
            send_sem=r.half_send.at[values],
            recv_sem=r.half_recv.at[values],
            device_id=peers["up"] if values else peers["y"],
            device_id_type=MESH,
        )

    pl.when(z < last)(lambda: send_kv(place, 0).start())
    pl.when(y == 0)(lambda: send_kv(place, 1).start())

    loads["w_query"].wait()
    for h in range(heads):
        wide = slice(h * head, (h + 1) * head)
        r.qp[:, wide] = dot(r.a[...], r.w_first[:, wide])
        for t in tiles:
            qp = r.qp[t, wide]
            q = turn(qp * inverse_rms(qp) * gain_q, r.cosine[t, :], r.sine[t, :])
            q = bf16(q * (scale * LOG2E))
            r.q[h * rows + t.start : h * rows + t.stop, :] = q
            r.qt[:, h * rows + t.start : h * rows + t.stop] = q.T

    columns = [slice(h * rows, (h + 1) * rows) for h in range(heads)]

    def visit(source):
        vt = r.kv[source, :, head : 2 * head].T
        mask = allowed(source)
        for here in columns:
            p = jnp.where(mask, jnp.exp2(dot(r.kv[source, :, 0:head], r.qt[:, here])), 0.0)
            total = jnp.sum(p, axis=0, keepdims=True)
            o = dot(vt, bf16(p))
            r.total[:, here] = r.total[:, here] + total
            r.ot[:, here] = r.ot[:, here] + o

    r.total[...] = jnp.zeros_like(r.total)
    r.ot[...] = jnp.zeros_like(r.ot)

    def take_column(back):
        mine = place - 2 * back

        @pl.when(back <= z)
        def _():
            send_kv(mine, 0).wait_recv()
            pl.when(z < last)(lambda: send_kv(mine, 0).start())
            pl.when(mine > 0)(lambda: send_kv(mine, 1).start())
            pl.when(mine == 0)(lambda: send_half(0).start())

    def attend(step, carry):
        at = step - 1 - y
        back = at // 2 + 1
        other = (at >= 0) & (lax.rem(at + 2, 2) == 1)
        source = jnp.where(at >= 0, place - 2 * back + jnp.where(other, 1 - 2 * y, 0), place - step)

        @pl.when((step == 1) & (y == 1))
        def _():
            send_kv(place - 1, 1).wait_recv()
            pl.when((z == 0) & (z < last))(lambda: send_half(1).start())

        pl.when(at == 0)(lambda: take_column(1))

        @pl.when(other)
        def _():
            take_column(back + 1)
            pl.when(source > 0)(lambda: send_kv(source, 1).wait_recv())

            @pl.when(source == 0)
            def _():
                send_half(1).wait_recv()
                pl.when(z < last)(lambda: send_half(1).start())
                send_half(0).wait_recv()

        visit(source)
        return carry

    lax.fori_loop(0, 1 + y + 2 * z, attend, 0)
    for h, here in enumerate(columns):
        total = r.total[:, here]
        o = r.ot[:, here] * (1.0 / total)
        r.lse[:, here] = jnp.log2(total)
        r.ot[:, here] = o
        r.ob[:, h * head : (h + 1) * head] = bf16(o).T

    loads["w_out"].wait()
    r.ap[...] = dot(r.ob[:, 0:joined], r.w_out[...])
    for t in tiles:
        ap = r.ap[t, :]
        x1 = f32(r.x[t, :]) + ap * inverse_rms(ap) * gain_attn
        r.x1[t, :] = x1
        r.m[t, :] = bf16(x1 * inverse_rms(x1) * gain_pre)
    loads["w_gate"].wait()
    loads["w_up"].wait()
    block = hidden // 8

    def quarters(body):
        def both(pair, carry):
            for quarter in (2 * pair, 2 * pair + 1):
                body(pl.ds(pl.multiple_of(quarter * 2 * block, 128), 2 * block))
            return carry

        lax.fori_loop(0, 2, both, 0)

    def feed(cols):
        gate = dot(r.m[...], r.w_pair[0, :, cols])
        up = dot(r.m[...], r.w_pair[1, :, cols])
        inner = 0.7978845608028654 * (gate + 0.044715 * gate * gate * gate)
        th = jnp.tanh(inner)
        cdf = 0.5 * (1.0 + th)
        act = gate * cdf
        slope = cdf + 0.5 * gate * (1.0 - th * th) * 0.7978845608028654 * (1.0 + 3 * 0.044715 * gate * gate)
        r.hid[:, cols] = bf16(act * up)
        r.side_gate[:, cols] = bf16(slope * up)
        r.side_up[:, cols] = bf16(act)

    quarters(feed)
    loads["w_down"].wait()
    loads["dy"].wait()
    r.wide[...] = dot(r.hid[...], r.w_down[...])
    r.gains[...] = jnp.zeros_like(r.gains)

    def gain(k, terms):
        r.gains[k, :, 0 : terms.shape[1]] = r.gains[k, :, 0 : terms.shape[1]] + terms

    for t in tiles:
        f = r.wide[t, :]
        inverse = inverse_rms(f)
        r.out[t, :] = bf16(r.x1[t, :] + f * inverse * gain_post)
        df, g = rms_back(f, inverse, gain_post, f32(r.dy[t, :]))
        r.df[t, :] = bf16(df)
        gain(3, g)
    def two_blocks(body):
        def both(pair, carry):
            for j in (2 * pair, 2 * pair + 1):
                body(j, pl.ds(pl.multiple_of(j * block, 128), block))
            return carry

        lax.fori_loop(0, 4, both, 0)

    def down_grad(j, cols):
        r.g_down[j] = bf16(dot_tn(r.hid[:, cols], r.df[...]))

    two_blocks(down_grad)

    chunks = []
    sems = (r.red_send, r.red_recv, r.red_local)
    for name, count in r_plan(sizes):
        grad, total = r["g_" + name], r["t_" + name]
        step = grad.shape[1] // count
        for i in range(count):
            number, kind = len(chunks), FIRST[len(chunks)]
            make, first = (LineChunk, {"u": "x", "v": "y"}[kind]) if kind in "uv" else (Chunk, kind)
            landing = tuple(r[f"land{k}_{number}"] for k in range(len(make.landing(step))))
            chunks.append(make(number, grad, total, i * step, step, first, landing, sems, me, peers, z_count))

    def side_grads(part):
        def one(cols):
            dh = dot_nt(r.df[...], r.w_down[cols, :])
            r.side_gate[:, cols] = bf16(dh * f32(r.side_gate[:, cols]))
            r.side_up[:, cols] = bf16(dh * f32(r.side_up[:, cols]))

        quarters(one)

    def feed_grads(part):
        grad, side = ((r.g_gate, r.side_gate), (r.g_up, r.side_up))[part]

        def one(j, cols):
            grad[j] = bf16(dot_tn(r.m[...], side[:, cols]))

        two_blocks(one)

    def middle_back(part):
        r.wide[...] = dot_nt(r.side_gate[...], r.w_pair[0]) + dot_nt(r.side_up[...], r.w_pair[1])
        for t in tiles:
            x1 = r.x1[t, :]
            dx1, g = rms_back(x1, inverse_rms(x1), gain_pre, r.wide[t, :])
            gain(2, g)
            dx1 = dx1 + f32(r.dy[t, :])
            r.x1[t, :] = dx1
            ap = r.ap[t, :]
            dap, g = rms_back(ap, inverse_rms(ap), gain_attn, dx1)
            gain(1, g)
            r.dap[t, :] = bf16(dap)

    def out_back(part):
        for h, here in enumerate(columns):
            wide = slice(h * head, (h + 1) * head)
            g = bf16(dot_tn(r.ob[:, wide], r.dap[...]))
            r.g_out[2 * h] = g[0:half]
            r.g_out[2 * h + 1] = g[half:head]
            do = bf16(dot_nt(r.dap[...], r.w_out[wide, :]))
            r.do[here, :] = do
            turned = do.T
            r.dot[:, here] = turned
            r.delta[:, here] = jnp.sum(f32(turned) * r.ot[:, here], axis=0, keepdims=True)
        r.ot[...] = jnp.zeros_like(r.ot)

    probs, dscores = r.hid.at[:, 0 : heads * rows], r.side_gate.at[:, 0 : heads * rows]

    def visit_back(source, target):
        kt = r.kv[source, :, 0:head].T
        mask = allowed(source)
        for here in columns:
            s = dot(r.kv[source, :, 0:head], r.qt[:, here])
            p = jnp.where(mask, jnp.exp2(s - r.lse[:, here]), 0.0)
            dp = dot(r.kv[source, :, head : 2 * head], r.dot[:, here])
            probs[:, here] = bf16(p)
            dscores[:, here] = bf16(p * (dp - r.delta[:, here]))
        target[:, 0:head] = bf16(dot(dscores[...], r.q[...]))
        target[:, head : 2 * head] = bf16(dot(probs[...], r.do[...]))
        for here in columns:
            r.ot[:, here] = r.ot[:, here] + dot(kt, dscores[:, here])

    def staged(own, row):
        return r.w_pair.at[own, 0:rows, row * 2 * head : (row + 1) * 2 * head]

    def to_partner(row):
        return pltpu.make_async_remote_copy(
            src_ref=staged(0, row),
            dst_ref=r.from_partner.at[row],
            send_sem=r.dkv_send.at[0, row],
            recv_sem=r.dkv_recv.at[0, row],
            device_id=peers["y"],
            device_id_type=MESH,
        )

    def to_below(row):
        return pltpu.make_async_remote_copy(
            src_ref=staged(1, row),
            dst_ref=r.from_above.at[row],
            send_sem=r.dkv_send.at[1, row],
            recv_sem=r.dkv_recv.at[1, row],
            device_id=peers["down"],
            device_id_type=MESH,
        )

    def visit_row(row):
        def one(own, carry):
            column = jnp.where(own == 1, y, 1 - y)

            @pl.when((row < z) | ((row == z) & (column <= y)))
            def _():
                visit_back(2 * row + column, staged(own, row))
                pl.when(own == 0)(lambda: to_partner(row).start())

            return carry

        lax.fori_loop(0, 2, one, 0)

    def pass_down(row):
        @pl.when(row < z)
        def _():
            to_partner(row).wait_recv()
            pl.when(z < last)(lambda: to_below(row).wait_recv())
            for t in tiles:
                value = f32(staged(1, row)[t, :]) + f32(r.from_partner[row, t, :])
                above = jnp.where(z < last, f32(r.from_above[row, t, :]), 0.0)
                staged(1, row)[t, :] = bf16(value + above)
            to_below(row).start()

    def queries_back(h):
        wide = slice(h * head, (h + 1) * head)
        for t in tiles:
            dq = (r.ot[:, h * rows + t.start : h * rows + t.stop] * scale).T
            qp = r.qp[t, wide]
            dqp, g = rms_back(qp, inverse_rms(qp), gain_q, turn_back(dq, r.cosine[t, :], r.sine[t, :]))
            gain(4, g)
            r.ob[t, wide] = bf16(dqp)

    def query_grad(part):
        for h in range(heads):
            g = bf16(dot_tn(r.a[...], r.ob[:, h * head : (h + 1) * head]))
            r.g_query[2 * h] = g[:, 0:half]
            r.g_query[2 * h + 1] = g[:, half:head]

    def own_total(part):
        for row in range(z_count):

            @pl.when(row == z)
            def _():
                pl.when(y == 0)(lambda: to_partner(row).wait_recv())
                pl.when(z < last)(lambda: to_below(row).wait_recv())
                for t in tiles:
                    beside = jnp.where(y == 0, f32(r.from_partner[row, t, :]), 0.0)
                    above = jnp.where(z < last, f32(r.from_above[row, t, :]), 0.0)
                    r.dkv[t, :] = f32(staged(1, row)[t, :]) + beside + above

    def keys_back(part):
        for t in tiles:
            dk = r.dkv[t, 0:head] * LN2
            kp = r.kp[t, :]
            dkp, g = rms_back(kp, inverse_rms(kp), gain_k, turn_back(dk, r.cosine[t, :], r.sine[t, :]))
            gain(5, g)
            r.ob[t, wide_k] = bf16(dkp)
            r.ob[t, wide_v] = bf16(r.dkv[t, head : 2 * head])
        low = width // 2
        g = bf16(dot_tn(r.a[...], r.ob[:, joined : joined + 2 * head]))
        for p in range(8):
            which, upper, side = p // 4, (p // 2) % 2, p % 2
            left = which * head + side * half
            r.g_kv[p] = g[upper * low : (upper + 1) * low, left : left + half]
        r.wide[...] = dot_nt(r.ob[...], r.w_first[...])
        for t in tiles:
            x = f32(r.x[t, :])
            dx, g = rms_back(x, inverse_rms(x), gain_in, r.wide[t, :])
            gain(0, g)
            r.dx[t, :] = bf16(r.x1[t, :] + dx)
        r.g_gain[...] = jnp.zeros_like(r.g_gain)
        at = 0
        for k, size in enumerate((width, width, width, width, head, head)):
            g = jnp.sum(r.gains[k], axis=0, keepdims=True)
            for part in range(size // 128):
                r.g_gain[at // 16, at % 16 : at % 16 + 1, :] = g[:, part * 128 : (part + 1) * 128]
                at += 1

    work = {
        "S": side_grads,
        "F": feed_grads,
        "M": middle_back,
        "O": out_back,
        "V": visit_row,
        "P": pass_down,
        "Q": queries_back,
        "G": query_grad,
        "T": own_total,
        "K": keys_back,
    }
    for what, step in schedule:
        if what in work:
            work[what](step)
        else:
            chunks[what].tick(step)

    pl.when(z < last)(lambda: send_kv(place, 0).wait_send())
    pl.when(y == 0)(lambda: send_kv(place, 1).wait_send())
    pl.when((y == 1) & (z < last))(lambda: send_half(1).wait_send())
    pl.when((y == 0) & (z > 0))(lambda: send_half(0).wait_send())
    for back in range(1, z_count):

        @pl.when(back <= z)
        def _():
            mine = place - 2 * back
            pl.when(z < last)(lambda: send_kv(mine, 0).wait_send())
            pl.when(mine > 0)(lambda: send_kv(mine, 1).wait_send())

    for row in range(z_count):
        pl.when((row < z) | ((row == z) & (y == 1)))(lambda: to_partner(row).wait_send())
        pl.when(row < z)(lambda: to_below(row).wait_send())


def r_plan(sizes):
    return list(zip(("down", "gate", "up", "out", "query", "kv", "gain"), PIECES, strict=True))


def gradient_shapes(sizes):
    rows, width, hidden, heads, head, z_count = sizes
    joined, half = heads * head, head // 2
    return {
        "down": ((8, hidden // 8, width), (8, hidden // 8, width)),
        "gate": ((8, width, hidden // 8), (width, hidden)),
        "up": ((8, width, hidden // 8), (width, hidden)),
        "out": ((8, joined // 8, width), (8, joined // 8, width)),
        "query": ((8, width, joined // 8), (width, joined)),
        "kv": ((8, width // 2, half), (2, 2, width // 2, head)),
        "gain": ((8, 16, 128), (8, 16, 128)),
    }


def layer_scratch(sizes):
    rows, width, hidden, heads, head, z_count = sizes
    joined = heads * head
    low, wide = jnp.bfloat16, jnp.float32
    arrays = {
        "x": ((rows, width), low),
        "w_first": ((width, joined + 2 * head), low),
        "w_out": ((joined, width), low),
        "w_pair": ((2, width, hidden), low),
        "w_down": ((hidden, width), low),
        "dy": ((rows, width), low),
        "a": ((rows, width), low),
        "gains": ((6, 8, width), wide),
        "kp": ((rows, head), wide),
        "kv": ((2 * z_count, rows, 2 * head), low),
        "qp": ((rows, joined), wide),
        "q": ((heads * rows, head), low),
        "qt": ((head, heads * rows), low),
        "cosine": ((rows, head // 2), wide),
        "sine": ((rows, head // 2), wide),
        "wide": ((rows, width), wide),
        "ot": ((head, heads * rows), wide),
        "total": ((1, heads * rows), wide),
        "lse": ((1, heads * rows), wide),
        "delta": ((1, heads * rows), wide),
        "ob": ((rows, joined + 2 * head), low),
        "ap": ((rows, width), wide),
        "x1": ((rows, width), wide),
        "m": ((rows, width), low),
        "hid": ((rows, hidden), low),
        "side_gate": ((rows, hidden), low),
        "side_up": ((rows, hidden), low),
        "df": ((rows, width), low),
        "dap": ((rows, width), low),
        "do": ((heads * rows, head), low),
        "dot": ((head, heads * rows), low),
        "dkv": ((rows, 2 * head), wide),
        "from_partner": ((z_count, rows, 2 * head), low),
        "from_above": ((z_count, rows, 2 * head), low),
    }
    shapes = gradient_shapes(sizes)
    pieces = 0
    for name, count in r_plan(sizes):
        (eight, high, columns), kind = shapes[name][0], wide if name == "gain" else low
        step = high // count
        pieces += count
        arrays["g_" + name] = (shapes[name][0], kind)
        for number in range(pieces - count, pieces):
            for k, shape in enumerate(LineChunk.landing(step) if FIRST[number] in "uv" else Chunk.landing(step)):
                arrays[f"land{k}_{number}"] = (shape + (columns,), kind)
    sems = {
        "load_sem": (9,),
        "kv_send": (2, 2 * z_count),
        "kv_recv": (2 * z_count,),
        "half_send": (2,),
        "half_recv": (2,),
        "dkv_send": (2, z_count),
        "dkv_recv": (2, z_count),
        "red_send": (pieces, STAGES),
        "red_recv": (pieces, STAGES),
        "red_local": (pieces,),
    }
    return arrays, sems


def layer_bytes(sizes):
    total = 0
    for shape, kind in layer_scratch(sizes)[0].values():
        size = jnp.dtype(kind).itemsize
        for n in shape[:-2]:
            size *= n
        total += size * max(shape[-2], 8) * max(shape[-1], 128)
    return total


VMEM_BYTES = 64 * 2**20


def widen_kernel(count, *refs):
    ins, table, both, tokens = refs[: count - 2], refs[count - 2], refs[count - 1], refs[count : count + 2]
    refs = refs[count + 2 :]
    outs, gains, tokens_out = refs[:count], refs[count : count + 6], refs[count + 6 : count + 8]
    refs = refs[count + 8 :]
    narrow, broad, (came, gone) = refs[: count + 2], refs[count + 2 : 2 * count + 2], refs[2 * count + 2 :]
    ins = (both.at[0], both.at[1]) + ins + tokens
    outs = outs + tokens_out
    loads = [pltpu.make_async_copy(ins[i], narrow[i], came.at[i]) for i in range(count + 2)]
    stores = [pltpu.make_async_copy((broad + narrow[count:])[i], outs[i], gone.at[i]) for i in range(count + 2)]
    for item in loads:
        item.start()
    at = 0
    for gain in gains:
        for part in range(gain.shape[0] // 128):
            gain[part * 128 : (part + 1) * 128] = table[at // 16, at % 16, :]
            at += 1
    for i in range(count):
        loads[i].wait()

        def body(j, carry):
            here = pl.ds(pl.multiple_of(j * 32, 32), 32)
            broad[i][here, :] = f32(narrow[i][here, :])
            return carry

        lax.fori_loop(0, narrow[i].shape[0] // 32, body, 0)
        stores[i].start()
    for i in (count, count + 1):
        loads[i].wait()
        stores[i].start()
    for item in stores:
        item.wait()


def widen(both, matrices, table, tokens, gain_sizes):
    count = len(matrices) + 2
    shapes = [both.shape[1:]] * 2 + [v.shape for v in matrices]
    anywhere, vmem = pl.BlockSpec(memory_space=pl.ANY), pl.BlockSpec(memory_space=pltpu.VMEM)
    return pl.pallas_call(
        functools.partial(widen_kernel, count),
        out_shape=tuple(jax.ShapeDtypeStruct(shape, jnp.float32) for shape in shapes)
        + tuple(jax.ShapeDtypeStruct((n,), jnp.float32) for n in gain_sizes)
        + tuple(jax.ShapeDtypeStruct(v.shape, v.dtype) for v in tokens),
        in_specs=[anywhere] * len(matrices) + [vmem] + [anywhere] * 3,
        out_specs=tuple([anywhere] * count + [vmem] * len(gain_sizes) + [anywhere] * 2),
        scratch_shapes=[pltpu.VMEM(shape, jnp.bfloat16) for shape in shapes + [v.shape for v in tokens]]
        + [pltpu.VMEM(shape, jnp.float32) for shape in shapes]
        + [pltpu.SemaphoreType.DMA((count + 2,))] * 2,
        compiler_params=pltpu.CompilerParams(vmem_limit_bytes=VMEM_BYTES),
    )(*matrices, table, both, *tokens)


def whole_layer(sizes, tokens, lengths, cotangent, norm_in, w_query, w_key, w_value, query_gain, key_gain, w_out, norm_attn, norm_pre, w_gate, w_up, w_down, norm_post):
    rows, width, hidden, heads, head, z_count = sizes
    joined = heads * head
    inputs = {
        "lengths": lengths,
        "norm_in": norm_in,
        "query_gain": query_gain,
        "key_gain": key_gain,
        "norm_attn": norm_attn,
        "norm_pre": norm_pre,
        "norm_post": norm_post,
        "x_in": tokens[0],
        "w_key_in": w_key,
        "w_value_in": w_value,
        "w_query_in": w_query,
        "w_out_in": w_out,
        "w_gate_in": w_gate,
        "w_up_in": w_up,
        "w_down_in": w_down,
        "dy_in": cotangent[0],
    }
    spaces = {name: pltpu.SMEM if name == "lengths" else pl.ANY if name.endswith("_in") and name != "norm_in" else pltpu.VMEM for name in inputs}
    shapes = gradient_shapes(sizes)
    outputs = {"out": (rows, width), "dx": (rows, width)}
    outputs.update({"t_" + name: shapes[name][1] for name in shapes})
    arrays, sems = layer_scratch(sizes)
    names = list(inputs) + list(outputs) + list(arrays) + list(sems)
    results = pl.pallas_call(
        functools.partial(layer_kernel, sizes, SCHEDULES[z_count], names),
        out_shape=tuple(
            jax.ShapeDtypeStruct(shape, jnp.float32 if name == "t_gain" else jnp.bfloat16) for name, shape in outputs.items()
        ),
        in_specs=[pl.BlockSpec(memory_space=spaces[name]) for name in inputs],
        out_specs=tuple(
            pl.BlockSpec(memory_space=pl.ANY if name.startswith("t_") else pltpu.VMEM) for name in outputs
        ),
        scratch_shapes=[pltpu.VMEM(*item) for item in arrays.values()]
        + [pltpu.SemaphoreType.DMA(item) for item in sems.values()],
        compiler_params=pltpu.CompilerParams(
            collective_id=1, has_side_effects=True, vmem_limit_bytes=VMEM_BYTES
        ),
    )(*inputs.values())
    r = Names(zip(outputs, results, strict=True))
    matrices = [
        r.t_query,
        r.t_out.reshape(joined, width),
        r.t_gate,
        r.t_up,
        r.t_down.reshape(hidden, width),
    ]
    both = r.t_kv.reshape(2, width, head)
    sums = widen(both, matrices, r.t_gain, (r.out, r.dx), (width, width, width, width, head, head))
    g_key, g_value, g_query, g_out, g_gate, g_up, g_down = sums[:7]
    g_in, g_attn, g_pre, g_post, g_qgain, g_kgain, output, input_grad = sums[7:]
    return (
        output[None],
        input_grad[None],
        g_in,
        g_query,
        g_key,
        g_value,
        g_qgain,
        g_kgain,
        g_out,
        g_attn,
        g_pre,
        g_gate,
        g_up,
        g_down,
        g_post,
    )


def per_device(
    tokens,
    lengths,
    cotangent,
    norm_in,
    w_query,
    w_key,
    w_value,
    query_gain,
    key_gain,
    w_out,
    norm_attn,
    norm_pre,
    w_gate,
    w_up,
    w_down,
    norm_post,
):
    rows = tokens.shape[1]
    head = query_gain.shape[0]
    heads = w_query.shape[1] // head
    sizes = (rows, tokens.shape[2], w_gate.shape[1], heads, head, lax.axis_size(BLOCKS) // 2)
    if sizes[-1] in SCHEDULES and layer_bytes(sizes) <= VMEM_BYTES:
        return whole_layer(
            sizes,
            tokens,
            lengths,
            cotangent,
            norm_in,
            w_query,
            w_key,
            w_value,
            query_gain,
            key_gain,
            w_out,
            norm_attn,
            norm_pre,
            w_gate,
            w_up,
            w_down,
            norm_post,
        )
    scale = head ** (-0.5)
    count = lax.axis_size(BLOCKS)
    place = lax.axis_index(BLOCKS)
    row = lengths[0]
    local_idx = place * rows + jnp.arange(rows, dtype=jnp.int32)
    seg_q, pos_q = segment_of(local_idx, row)
    cosine, sine = rotary_tables(pos_q, head)

    def block_mask(source):
        key_idx = source * rows + jnp.arange(rows, dtype=jnp.int32)
        seg_k, unused = segment_of(key_idx, row)
        return (seg_q[:, None] == seg_k[None, :]) & (local_idx[:, None] >= key_idx[None, :])

    x_in = tokens[0].astype(jnp.float32)
    normal_a = normed(x_in, norm_in).astype(jnp.bfloat16)
    q_proj = jnp.dot(normal_a, w_query, preferred_element_type=jnp.float32).reshape(
        rows, heads, head
    )
    k_proj = jnp.dot(normal_a, w_key, preferred_element_type=jnp.float32)
    v_proj = jnp.dot(normal_a, w_value, preferred_element_type=jnp.float32)
    query = prepare(q_proj, query_gain, cosine[:, None, :], sine[:, None, :]).astype(jnp.bfloat16)
    keys = prepare(k_proj, key_gain, cosine, sine).astype(jnp.bfloat16)
    values = v_proj.astype(jnp.bfloat16)
    q_heads = jnp.transpose(query, (1, 0, 2))

    def absorb(state, pair, source):
        allowed = block_mask(source)
        big, total, accum = state
        raw = jnp.einsum("hqd,kd->hqk", q_heads, pair[0], preferred_element_type=jnp.float32)
        scores = jnp.where(allowed[None], scale * raw, NEG)
        big_new = jnp.maximum(big, jnp.max(scores, axis=-1, keepdims=True))
        expo = jnp.where(allowed[None], jnp.exp(scores - big_new), 0.0)
        fade = jnp.exp(big - big_new)
        total = total * fade + jnp.sum(expo, axis=-1, keepdims=True)
        accum = accum * fade + jnp.einsum(
            "hqk,kd->hqd", expo.astype(jnp.bfloat16), pair[1], preferred_element_type=jnp.float32
        )
        return (big_new, total, accum)

    pair = jnp.stack([keys, values])
    state = (
        jnp.full((heads, rows, 1), NEG, jnp.float32),
        jnp.zeros((heads, rows, 1), jnp.float32),
        jnp.zeros((heads, rows, head), jnp.float32),
    )
    state = absorb(state, pair, place)

    def cycle_forward(step, carry):
        inner, moving = carry
        moving = from_behind(moving, BLOCKS, 1)
        return (absorb(inner, moving, (place - step) % count), moving)

    state, unused_pair = lax.fori_loop(1, count, cycle_forward, (state, pair))
    big, total, accum = state
    attended = accum / total
    lse = big + jnp.log(total)
    joined = jnp.transpose(attended, (1, 0, 2)).reshape(rows, heads * head).astype(jnp.bfloat16)
    a_proj = jnp.dot(joined, w_out, preferred_element_type=jnp.float32)
    x_mid = x_in + normed(a_proj, norm_attn)
    mixed = normed(x_mid, norm_pre).astype(jnp.bfloat16)
    gate = jnp.dot(mixed, w_gate, preferred_element_type=jnp.float32)
    upper = jnp.dot(mixed, w_up, preferred_element_type=jnp.float32)

    def activate(gate_in, upper_in):
        return jax.nn.gelu(gate_in, approximate=True) * upper_in

    hidden = activate(gate, upper).astype(jnp.bfloat16)
    f_proj = jnp.dot(hidden, w_down, preferred_element_type=jnp.float32)
    output = x_mid + normed(f_proj, norm_post)
    grad_y = cotangent[0].astype(jnp.float32)
    d_fproj, g_post = normed_back(f_proj, norm_post, grad_y)
    d_fproj = d_fproj.astype(jnp.bfloat16)
    g_down = dot_tn(hidden, d_fproj)
    d_hidden = dot_nt(d_fproj, w_down)
    d_gate, d_upper = jax.vjp(activate, gate, upper)[1](d_hidden)
    d_gate = d_gate.astype(jnp.bfloat16)
    d_upper = d_upper.astype(jnp.bfloat16)
    g_gate = dot_tn(mixed, d_gate)
    g_up = dot_tn(mixed, d_upper)
    d_mixed = dot_nt(d_gate, w_gate) + dot_nt(d_upper, w_up)
    d_mid, g_pre = normed_back(x_mid, norm_pre, d_mixed)
    d_mid = grad_y + d_mid
    d_aproj, g_attn = normed_back(a_proj, norm_attn, d_mid)
    d_aproj = d_aproj.astype(jnp.bfloat16)
    g_out = dot_tn(joined, d_aproj)
    d_joined = dot_nt(d_aproj, w_out).astype(
        jnp.bfloat16
    )
    do_heads = jnp.transpose(d_joined.reshape(rows, heads, head), (1, 0, 2))
    delta = jnp.sum(do_heads.astype(jnp.float32) * attended, axis=-1, keepdims=True)

    def visit(d_query, moving, grads, source):
        allowed = block_mask(source)
        raw = jnp.einsum("hqd,kd->hqk", q_heads, moving[0], preferred_element_type=jnp.float32)
        probs = jnp.where(allowed[None], jnp.exp(scale * raw - lse), 0.0)
        dv_add = jnp.einsum(
            "hqk,hqd->kd", probs.astype(jnp.bfloat16), do_heads, preferred_element_type=jnp.float32
        )
        d_probs = jnp.einsum("hqd,kd->hqk", do_heads, moving[1], preferred_element_type=jnp.float32)
        d_scores = (scale * probs * (d_probs - delta)).astype(jnp.bfloat16)
        dq_add = jnp.einsum("hqk,kd->hqd", d_scores, moving[0], preferred_element_type=jnp.float32)
        dk_add = jnp.einsum("hqk,hqd->kd", d_scores, q_heads, preferred_element_type=jnp.float32)
        return (d_query + dq_add, grads + jnp.stack([dk_add, dv_add]))

    d_query = jnp.zeros((heads, rows, head), jnp.float32)
    grads = jnp.zeros((2, rows, head), jnp.float32)
    d_query, grads = visit(d_query, pair, grads, place)

    def cycle_backward(step, carry):
        dq_in, moving, grads_in = carry
        moving = from_behind(moving, BLOCKS, 1)
        grads_in = pass_home(grads_in)
        dq_in, grads_in = visit(dq_in, moving, grads_in, (place - step) % count)
        return (dq_in, moving, grads_in)

    d_query, unused_pair, grads = lax.fori_loop(1, count, cycle_backward, (d_query, pair, grads))
    grads = pass_home(grads)

    def query_piece(proj, gain):
        return prepare(proj, gain, cosine[:, None, :], sine[:, None, :])

    def key_piece(proj, gain):
        return prepare(proj, gain, cosine, sine)

    d_qproj, g_qgain = jax.vjp(query_piece, q_proj, query_gain)[1](
        jnp.transpose(d_query, (1, 0, 2))
    )
    d_kproj, g_kgain = jax.vjp(key_piece, k_proj, key_gain)[1](grads[0])
    d_qproj = d_qproj.reshape(rows, heads * head).astype(jnp.bfloat16)
    d_kproj = d_kproj.astype(jnp.bfloat16)
    d_vproj = grads[1].astype(jnp.bfloat16)
    g_query = dot_tn(normal_a, d_qproj)
    g_key = dot_tn(normal_a, d_kproj)
    g_value = dot_tn(normal_a, d_vproj)
    d_normal = dot_nt(d_qproj, w_query)
    d_normal = d_normal + dot_nt(d_kproj, w_key)
    d_normal = d_normal + dot_nt(d_vproj, w_value)
    d_input, g_in = normed_back(x_in, norm_in, d_normal)
    input_grad = (d_mid + d_input).astype(jnp.bfloat16)
    (
        g_in,
        g_query,
        g_key,
        g_value,
        g_qgain,
        g_kgain,
        g_out,
        g_attn,
        g_pre,
        g_gate,
        g_up,
        g_down,
        g_post,
    ) = sum_gradients(
        (
            g_in,
            g_query,
            g_key,
            g_value,
            g_qgain,
            g_kgain,
            g_out,
            g_attn,
            g_pre,
            g_gate,
            g_up,
            g_down,
            g_post,
        )
    )
    return (
        output.astype(jnp.bfloat16)[None],
        input_grad[None],
        g_in,
        g_query,
        g_key,
        g_value,
        g_qgain,
        g_kgain,
        g_out,
        g_attn,
        g_pre,
        g_gate,
        g_up,
        g_down,
        g_post,
    )


def solution(mesh):
    in_specs = (
        P(PARTS, BLOCKS, None),
        P(PARTS, None),
        P(PARTS, BLOCKS, None),
        P(),
        P(),
        P(),
        P(),
        P(),
        P(),
        P(),
        P(),
        P(),
        P(),
        P(),
        P(),
        P(),
    )
    out_specs = (
        P(PARTS, BLOCKS, None),
        P(PARTS, BLOCKS, None),
        P(),
        P(),
        P(),
        P(),
        P(),
        P(),
        P(),
        P(),
        P(),
        P(),
        P(),
        P(),
        P(),
    )
    return jax.shard_map(
        per_device, mesh=mesh, in_specs=in_specs, out_specs=out_specs, check_vma=False
    )
```

profile of v0, /device:TPU:0, one launch (start us, length us, event | category | flops | bytes accessed | tf_op | source)
XLA Modules:
  0.0 191.8 jit_solution(3187665483742777222)
XLA Ops:
  0.7 177.5 %shard_map.271 = (bf16[384,640]{1,0:T(8,128)(2,1)}, bf16[384,640]{1,0:T(8,128)(2,1)}, bf16[8,256,640]{2,1,0:T(8,128)(2,1)}, bf16[640,2048]{1,0:T(8,128)(2,1)}, b...) custom-call(s32[1,4]{1,0:T(1,128)} %refs_0_.1, ...), custom_call_target="tpu_custom_call" | custom-call | tf_op jit(solution)/shard_map/pallas_call | solution.py:1344
  178.1 13.5 %shard_map.272 = (f32[640,256]{1,0:T(8,128)}, f32[640,256]{1,0:T(8,128)}, f32[640,1024]{1,0:T(8,128)}, f32[1024,640]{1,0:T(8,128)}, f32[640,2048]{1,0:T(8,128)},...) custom-call(bf16[640,1024]{1,0:T(8,128)(2,1)} %get-tuple-element.39., ...), custom_call_target="tpu_custom_call" | custom-call | tf_op jit(solution)/shard_map/pallas_call | solution.py:1303
where the time goes:
time: 192 us
  Pallas kernels  191 us (99%)
    pallas_call x1, Pallas kernels, whole_layer(): pl.pallas_call(functools.partial(layer_kernel, sizes, SCHEDULES[z_count],...  177 us
    pallas_call x1, Pallas kernels, widen(): pl.pallas_call(functools.partial(widen_kernel, count), out_shape=tuple((j...  13.5 us

commit v1 on v0

--- a/solution.py
+++ b/solution.py
@@ -102,8 +102,10 @@
     def _():
         pl.semaphore_signal(barrier, inc=1, device_id=peers["down"], device_id_type=MESH)
 
+
+def meet(me, z_count):
     ends = (me["z"] == 0).astype(jnp.int32) + (me["z"] == z_count - 1).astype(jnp.int32)
-    pl.semaphore_wait(barrier, 5 - ends)
+    pl.semaphore_wait(pltpu.get_barrier_semaphore(), 5 - ends)
 
 
 def add_into(target, start, row, extra, count, rows):
@@ -564,6 +566,7 @@
     for item in loads:
         item.start()
     greet(me, peers, z_count)
+    meet(me, z_count)
     for item in loads:
         item.wait()
     chunks = []
@@ -826,6 +829,7 @@
             device_id_type=MESH,
         )
 
+    meet(me, z_count)
     pl.when(z < last)(lambda: send_kv(place, 0).start())
     pl.when(y == 0)(lambda: send_kv(place, 1).start())
 
@@ -1262,36 +1266,39 @@
 VMEM_BYTES = 64 * 2**20
 
 
-def widen_kernel(count, *refs):
-    ins, table, both, tokens = refs[: count - 2], refs[count - 2], refs[count - 1], refs[count : count + 2]
+def widen_kernel(count, gain_sizes, *refs):
+    ins, table_in, both, tokens = refs[: count - 2], refs[count - 2], refs[count - 1], refs[count : count + 2]
     refs = refs[count + 2 :]
-    outs, gains, tokens_out = refs[:count], refs[count : count + 6], refs[count + 6 : count + 8]
+    outs, gains_out, tokens_out = refs[:count], refs[count : count + 6], refs[count + 6 : count + 8]
     refs = refs[count + 8 :]
-    narrow, broad, (came, gone) = refs[: count + 2], refs[count + 2 : 2 * count + 2], refs[2 * count + 2 :]
-    ins = (both.at[0], both.at[1]) + ins + tokens
-    outs = outs + tokens_out
-    loads = [pltpu.make_async_copy(ins[i], narrow[i], came.at[i]) for i in range(count + 2)]
-    stores = [pltpu.make_async_copy((broad + narrow[count:])[i], outs[i], gone.at[i]) for i in range(count + 2)]
+    narrow, broad, gains, (table, came, gone) = refs[: count + 2], refs[count + 2 : 2 * count + 2], refs[2 * count + 2 : 2 * count + 8], refs[2 * count + 8 :]
+    ins = (both.at[0], both.at[1]) + ins + tokens + (table_in,)
+    outs = outs + tokens_out + gains_out
+    held = broad + narrow[count:] + gains
+    loads = [pltpu.make_async_copy(ins[i], (narrow + (table,))[i], came.at[i]) for i in range(count + 3)]
+    stores = [pltpu.make_async_copy(held[i], outs[i], gone.at[i]) for i in range(count + 8)]
     for item in loads:
         item.start()
-    at = 0
-    for gain in gains:
-        for part in range(gain.shape[0] // 128):
-            gain[part * 128 : (part + 1) * 128] = table[at // 16, at % 16, :]
-            at += 1
     for i in range(count):
         loads[i].wait()
 
         def body(j, carry):
-            here = pl.ds(pl.multiple_of(j * 32, 32), 32)
+            here = pl.ds(pl.multiple_of(j * 64, 64), 64)
             broad[i][here, :] = f32(narrow[i][here, :])
             return carry
 
-        lax.fori_loop(0, narrow[i].shape[0] // 32, body, 0)
+        lax.fori_loop(0, narrow[i].shape[0] // 64, body, 0)
         stores[i].start()
     for i in (count, count + 1):
         loads[i].wait()
         stores[i].start()
+    loads[count + 2].wait()
+    at = 0
+    for i, gain in enumerate(gains):
+        for part in range(gain_sizes[i] // 128):
+            gain[part * 128 : (part + 1) * 128] = table[at // 16, at % 16, :]
+            at += 1
+        stores[count + 2 + i].start()
     for item in stores:
         item.wait()
 
@@ -1299,17 +1306,19 @@
 def widen(both, matrices, table, tokens, gain_sizes):
     count = len(matrices) + 2
     shapes = [both.shape[1:]] * 2 + [v.shape for v in matrices]
-    anywhere, vmem = pl.BlockSpec(memory_space=pl.ANY), pl.BlockSpec(memory_space=pltpu.VMEM)
+    anywhere = pl.BlockSpec(memory_space=pl.ANY)
     return pl.pallas_call(
-        functools.partial(widen_kernel, count),
+        functools.partial(widen_kernel, count, gain_sizes),
         out_shape=tuple(jax.ShapeDtypeStruct(shape, jnp.float32) for shape in shapes)
         + tuple(jax.ShapeDtypeStruct((n,), jnp.float32) for n in gain_sizes)
         + tuple(jax.ShapeDtypeStruct(v.shape, v.dtype) for v in tokens),
-        in_specs=[anywhere] * len(matrices) + [vmem] + [anywhere] * 3,
-        out_specs=tuple([anywhere] * count + [vmem] * len(gain_sizes) + [anywhere] * 2),
+        in_specs=[anywhere] * (count + 2),
+        out_specs=tuple([anywhere] * (count + len(gain_sizes) + 2)),
         scratch_shapes=[pltpu.VMEM(shape, jnp.bfloat16) for shape in shapes + [v.shape for v in tokens]]
         + [pltpu.VMEM(shape, jnp.float32) for shape in shapes]
-        + [pltpu.SemaphoreType.DMA((count + 2,))] * 2,
+        + [pltpu.VMEM((n,), jnp.float32) for n in gain_sizes]
+        + [pltpu.VMEM(table.shape, table.dtype)]
+        + [pltpu.SemaphoreType.DMA((count + 3,)), pltpu.SemaphoreType.DMA((count + 8,))],
         compiler_params=pltpu.CompilerParams(vmem_limit_bytes=VMEM_BYTES),
     )(*matrices, table, both, *tokens)
 

time: 192 us -> 190 us (0.990)
  Pallas kernels: 191 us -> 189 us
where the time goes in v1:
time: 190 us
  Pallas kernels  189 us (99%)
    pallas_call x1, Pallas kernels, whole_layer(): pl.pallas_call(functools.partial(layer_kernel, sizes, SCHEDULES[z_count],...  177 us
    pallas_call x1, Pallas kernels, widen(): pl.pallas_call(functools.partial(widen_kernel, count, gain_sizes), out_sh...  11.8 us

profile of v1, /device:TPU:0, one launch (start us, length us, event | category | flops | bytes accessed | tf_op | source)
XLA Modules:
  0.0 189.6 jit_solution(2050947471421761490)
XLA Ops:
  0.7 176.9 %shard_map.271 = (bf16[384,640]{1,0:T(8,128)(2,1)}, bf16[384,640]{1,0:T(8,128)(2,1)}, bf16[8,256,640]{2,1,0:T(8,128)(2,1)}, bf16[640,2048]{1,0:T(8,128)(2,1)}, b...) custom-call(s32[1,4]{1,0:T(1,128)} %refs_0_.1, ...), custom_call_target="tpu_custom_call" | custom-call | tf_op jit(solution)/shard_map/pallas_call | solution.py:1353
  177.6 11.8 %shard_map.272 = (f32[640,256]{1,0:T(8,128)}, f32[640,256]{1,0:T(8,128)}, f32[640,1024]{1,0:T(8,128)}, f32[1024,640]{1,0:T(8,128)}, f32[640,2048]{1,0:T(8,128)},...) custom-call(bf16[640,1024]{1,0:T(8,128)(2,1)} %get-tuple-element.39., ...), custom_call_target="tpu_custom_call" | custom-call | tf_op jit(solution)/shard_map/pallas_call | solution.py:1310

commit v2 on v1

--- a/solution.py
+++ b/solution.py
@@ -947,7 +947,7 @@
     for t in tiles:
         f = r.wide[t, :]
         inverse = inverse_rms(f)
-        r.out[t, :] = bf16(r.x1[t, :] + f * inverse * gain_post)
+        r.out_held[t, :] = bf16(r.x1[t, :] + f * inverse * gain_post)
         df, g = rms_back(f, inverse, gain_post, f32(r.dy[t, :]))
         r.df[t, :] = bf16(df)
         gain(3, g)
@@ -958,6 +958,12 @@
             return carry
 
         lax.fori_loop(0, 4, both, 0)
+
+    leaving = [
+        pltpu.make_async_copy(r.out_held, r.out, r.load_sem.at[len(weights)]),
+        pltpu.make_async_copy(r.dx_held, r.dx, r.load_sem.at[len(weights) + 1]),
+    ]
+    leaving[0].start()
 
     def down_grad(j, cols):
         r.g_down[j] = bf16(dot_tn(r.hid[:, cols], r.df[...]))
@@ -1126,7 +1132,8 @@
             x = f32(r.x[t, :])
             dx, g = rms_back(x, inverse_rms(x), gain_in, r.wide[t, :])
             gain(0, g)
-            r.dx[t, :] = bf16(r.x1[t, :] + dx)
+            r.dx_held[t, :] = bf16(r.x1[t, :] + dx)
+        leaving[1].start()
         r.g_gain[...] = jnp.zeros_like(r.g_gain)
         at = 0
         for k, size in enumerate((width, width, width, width, head, head)):
@@ -1153,6 +1160,8 @@
         else:
             chunks[what].tick(step)
 
+    for item in leaving:
+        item.wait()
     pl.when(z < last)(lambda: send_kv(place, 0).wait_send())
     pl.when(y == 0)(lambda: send_kv(place, 1).wait_send())
     pl.when((y == 1) & (z < last))(lambda: send_half(1).wait_send())
@@ -1200,6 +1209,8 @@
         "w_down": ((hidden, width), low),
         "dy": ((rows, width), low),
         "a": ((rows, width), low),
+        "out_held": ((rows, width), low),
+        "dx_held": ((rows, width), low),
         "gains": ((6, 8, width), wide),
         "kp": ((rows, head), wide),
         "kv": ((2 * z_count, rows, 2 * head), low),
@@ -1239,7 +1250,7 @@
             for k, shape in enumerate(LineChunk.landing(step) if FIRST[number] in "uv" else Chunk.landing(step)):
                 arrays[f"land{k}_{number}"] = (shape + (columns,), kind)
     sems = {
-        "load_sem": (9,),
+        "load_sem": (11,),
         "kv_send": (2, 2 * z_count),
         "kv_recv": (2 * z_count,),
         "half_send": (2,),
@@ -1277,9 +1288,10 @@
     held = broad + narrow[count:] + gains
     loads = [pltpu.make_async_copy(ins[i], (narrow + (table,))[i], came.at[i]) for i in range(count + 3)]
     stores = [pltpu.make_async_copy(held[i], outs[i], gone.at[i]) for i in range(count + 8)]
-    for item in loads:
-        item.start()
-    for i in range(count):
+    order = (*range(2, count), 0, 1)
+    for i in (*order, *range(count, count + 3)):
+        loads[i].start()
+    for i in order:
         loads[i].wait()
 
         def body(j, carry):
@@ -1357,7 +1369,7 @@
         ),
         in_specs=[pl.BlockSpec(memory_space=spaces[name]) for name in inputs],
         out_specs=tuple(
-            pl.BlockSpec(memory_space=pl.ANY if name.startswith("t_") else pltpu.VMEM) for name in outputs
+            pl.BlockSpec(memory_space=pl.ANY) for name in outputs
         ),
         scratch_shapes=[pltpu.VMEM(*item) for item in arrays.values()]
         + [pltpu.SemaphoreType.DMA(item) for item in sems.values()],

time: 190 us -> 189 us (level)
  Pallas kernels: 189 us -> 187 us
where the time goes in v2:
time: 189 us; the launch traced here: 188 us
  Pallas kernels  187 us (99%)
    pallas_call x1, Pallas kernels, whole_layer(): pl.pallas_call(functools.partial(layer_kernel, sizes, SCHEDULES[z_count],...  176 us
    pallas_call x1, Pallas kernels, widen(): pl.pallas_call(functools.partial(widen_kernel, count, gain_sizes), out_sh...  11.4 us

profile of v2, /device:TPU:0, one launch (start us, length us, event | category | flops | bytes accessed | tf_op | source)
XLA Modules:
  0.0 188.3 jit_solution(8626665287277997493)
XLA Ops:
  0.7 176.1 %shard_map.271 = (bf16[384,640]{1,0:T(8,128)(2,1)}, bf16[384,640]{1,0:T(8,128)(2,1)}, bf16[8,256,640]{2,1,0:T(8,128)(2,1)}, bf16[640,2048]{1,0:T(8,128)(2,1)}, b...) custom-call(s32[1,4]{1,0:T(1,128)} %refs_0_.1, ...), custom_call_target="tpu_custom_call" | custom-call | tf_op jit(solution)/shard_map/pallas_call | solution.py:1365
  176.7 11.4 %shard_map.272 = (f32[640,256]{1,0:T(8,128)}, f32[640,256]{1,0:T(8,128)}, f32[640,1024]{1,0:T(8,128)}, f32[1024,640]{1,0:T(8,128)}, f32[640,2048]{1,0:T(8,128)},...) custom-call(bf16[640,1024]{1,0:T(8,128)(2,1)} %get-tuple-element.39., ...), custom_call_target="tpu_custom_call" | custom-call | tf_op jit(solution)/shard_map/pallas_call | solution.py:1322

commit v3 on v2

--- a/solution.py
+++ b/solution.py
@@ -675,8 +675,8 @@
         (4, 2), (2, 0), (7, 0), (5, 0), ("V", 1), (3, 2), (1, 3), (6, 0), (0, 3), ("V", 2), (2, 1), (5, 1), (0, 4), (1, 4), (4, 3), (4, 4), (7, 1),
         (1, 5), (0, 5), (4, 5), (6, 1), (3, 3), ("P", 0), ("P", 1), ("V", 3), (0, 6), (1, 6), ("P", 2), ("Q", 0), ("Q", 1), (7, 2), (4, 6), (5, 2),
         ("Q", 2), (1, 7), ("Q", 3), (6, 2), (3, 4), ("G", 0), (0, 7), (8, 0), (1, 8), (2, 2), (9, 0), (5, 3), ("T", 0), (8, 1), (4, 7), (7, 3),
-        ("K", 0), (4, 8), (1, 9), (0, 8), (5, 4), (10, 0), (6, 3), (7, 4), (9, 1), (12, 0), (3, 5), (8, 2), (6, 4), (5, 5), (7, 5), (2, 3), (10, 1),
-        (11, 0), (6, 5), (12, 1), (2, 4), (3, 6), (11, 1), (9, 2), (10, 2), (5, 6), (12, 2), (7, 6), (4, 9), (6, 6), (5, 7), (3, 7), (2, 5), (1, 10),
+        ("K", 0), (10, 0), (11, 0), (4, 8), (1, 9), (0, 8), (5, 4), (6, 3), (7, 4), (9, 1), ("I", 0), (12, 0), (3, 5), (8, 2), (6, 4), (5, 5), (7, 5), (2, 3), (10, 1),
+         (6, 5), (12, 1), (2, 4), (3, 6), (11, 1), (9, 2), (10, 2), (5, 6), (12, 2), (7, 6), (4, 9), (6, 6), (5, 7), (3, 7), (2, 5), (1, 10),
         (11, 2), (6, 7), (12, 3), (8, 3), (0, 9), (7, 7), (12, 4), (8, 4), (10, 3), (9, 3), (5, 8), (10, 4), (9, 4), (11, 3), (4, 10), (2, 6),
         (11, 4), (7, 8), (3, 8), (6, 8), (8, 5), (5, 9), (12, 5), (10, 5), (7, 9), (6, 9), (11, 5), (8, 6), (9, 5), (0, 10), (12, 6), (2, 7), (11, 6),
         (12, 7), (10, 6), (8, 7), (10, 7), (9, 6), (7, 10), (11, 7), (9, 7), (3, 9), (6, 10), (8, 8), (1, 11), (10, 8), (2, 8), (8, 9), (2, 9),
@@ -1127,6 +1127,8 @@
             which, upper, side = p // 4, (p // 2) % 2, p % 2
             left = which * head + side * half
             r.g_kv[p] = g[upper * low : (upper + 1) * low, left : left + half]
+
+    def input_back(part):
         r.wide[...] = dot_nt(r.ob[...], r.w_first[...])
         for t in tiles:
             x = f32(r.x[t, :])
@@ -1153,6 +1155,7 @@
         "G": query_grad,
         "T": own_total,
         "K": keys_back,
+        "I": input_back,
     }
     for what, step in schedule:
         if what in work:

time: 189 us -> 188 us (level)
  no operation moved by 1% of the time
where the time goes in v3:
time: 188 us
  Pallas kernels  187 us (99%)
    pallas_call x1, Pallas kernels, whole_layer(): pl.pallas_call(functools.partial(layer_kernel, sizes, SCHEDULES[z_count],...  176 us
    pallas_call x1, Pallas kernels, widen(): pl.pallas_call(functools.partial(widen_kernel, count, gain_sizes), out_sh...  11.4 us

profile of v3, /device:TPU:0, one launch (start us, length us, event | category | flops | bytes accessed | tf_op | source)
XLA Modules:
  0.0 188.0 jit_solution(5748876318559309293)
XLA Ops:
  0.7 175.7 %shard_map.271 = (bf16[384,640]{1,0:T(8,128)(2,1)}, bf16[384,640]{1,0:T(8,128)(2,1)}, bf16[8,256,640]{2,1,0:T(8,128)(2,1)}, bf16[640,2048]{1,0:T(8,128)(2,1)}, b...) custom-call(s32[1,4]{1,0:T(1,128)} %refs_0_.1, ...), custom_call_target="tpu_custom_call" | custom-call | tf_op jit(solution)/shard_map/pallas_call | solution.py:1368
  176.4 11.4 %shard_map.272 = (f32[640,256]{1,0:T(8,128)}, f32[640,256]{1,0:T(8,128)}, f32[640,1024]{1,0:T(8,128)}, f32[1024,640]{1,0:T(8,128)}, f32[640,2048]{1,0:T(8,128)},...) custom-call(bf16[640,1024]{1,0:T(8,128)(2,1)} %get-tuple-element.39., ...), custom_call_target="tpu_custom_call" | custom-call | tf_op jit(solution)/shard_map/pallas_call | solution.py:1325
